TPU v7x, 32 devices: a whole 2x2x4 slice. The times are simulated.
32 devices in a mesh: rows: 8 (over y, x, core), cols: 4 (over z).
Axes of the slice: x: 2, y: 2, z: 4, core: 2. Of those that a mesh axis runs over, the one named last changes fastest.
Arguments:
- blocks: float32 [32, 4, 16, 128, 128], P('rows', 'cols'), may hold values from -0.125 to 0.125
- ell_index: int32 [32, 4, 16], P('rows', 'cols'), may hold values from 0 to 31, as said below
- counts: int32 [32, 4], P('rows', 'cols'), may hold values from 4 to 16, as said below
- objective: float32 [16384], P('cols'), may hold values from -6 to 6
- lower_bound: float32 [16384], P('cols'), may hold values from -0.4 to -0.05
- upper_bound: float32 [16384], P('cols'), may hold values from 0.05 to 0.4
- var_kind: int32 [16384], P('cols'), may hold values from 0 to 2
- demand: float32 [32, 4096], P(None, 'rows'), may hold values from -6 to 6
- row_kind: int32 [4096], P('rows'), may hold values from 0 to 1
- step_size: float32 [32], replicated, may hold values from 0.2 to 0.5
- primal_weight: float32 [32], replicated, may hold values from 0.5 to 2
Outputs:
- primal: float32 [32, 16384], P(None, 'cols')
- dual_vector: float32 [32, 4096], P(None, 'rows')
- final_weight: float32 [32], replicated
Inputs may be any that keep to these rules, and one draw needn't show every extreme that they name: Slots in use: for each row block r and column group c, slots 0 to counts[r, c] - 1 are in use; slots from counts[r, c] on to 15 are padding, and their blocks and ell_index entries are ignored. `ell_index`: the slots of one row block in one column group name distinct column blocks of that group.
All inputs are finite; a program needn't handle non-finite values.
Results may differ from a plain program's by a relative error of at most 0.0002.
Values sent between devices are 32-bit elements; how exact they have to be, the bound alone decides.
A program may use at most 64 MiB of HBM per device.

v0:
```python
import jax
import jax.numpy as jnp
from jax import lax
from jax.sharding import PartitionSpec as P

ITERS = 4


epsilon = 1e-06
highest = lax.Precision.HIGHEST


def project_primal(values, var_kind, lower_bound, upper_bound):
    floored = jnp.maximum(values, lower_bound[None, :])
    boxed = jnp.minimum(floored, upper_bound[None, :])
    kinds = var_kind[None, :]
    return jnp.where(kinds == 0, values, jnp.where(kinds == 1, floored, boxed))


def project_dual(values, row_kind):
    return jnp.where(row_kind[None, :] == 1, jnp.maximum(values, 0.0), values)


def local(
    blocks,
    ell_index,
    counts,
    objective,
    lower_bound,
    upper_bound,
    var_kind,
    demand,
    row_kind,
    step_size,
    primal_weight,
):
    row_blocks = blocks.shape[0]
    slots = blocks.shape[2]
    width = blocks.shape[3]
    tiles = blocks.reshape(row_blocks, slots, width, width)
    slot_ids = ell_index.reshape(row_blocks, slots)
    in_use = counts.reshape(row_blocks)
    groups = objective.shape[0] // width
    scenarios = demand.shape[0]
    longest = jnp.max(in_use)
    group_ids = jnp.arange(groups, dtype=jnp.int32)

    def forward(field):
        field_blocks = field.reshape(scenarios, groups, width)

        def forward_add_slot(slot_pos, total):
            tile_now = lax.dynamic_index_in_dim(tiles, slot_pos, 1, keepdims=False)
            slot_cols = lax.dynamic_index_in_dim(slot_ids, slot_pos, 1, keepdims=False)
            live = (slot_pos < in_use).astype(jnp.float32)
            taken = jnp.take(field_blocks, slot_cols, axis=1) * live[None, :, None]
            return total + jnp.einsum("rij,srj->sri", tile_now, taken, precision=highest)

        start = jnp.zeros((scenarios, row_blocks, width), jnp.float32)
        total = lax.fori_loop(jnp.int32(0), longest, forward_add_slot, start)
        return total.reshape(scenarios, row_blocks * width)

    def backward(dual_values):
        row_values = dual_values.reshape(scenarios, row_blocks, width)

        def backward_add_slot(slot_pos, total):
            tile_now = lax.dynamic_index_in_dim(tiles, slot_pos, 1, keepdims=False)
            slot_cols = lax.dynamic_index_in_dim(slot_ids, slot_pos, 1, keepdims=False)
            live = (slot_pos < in_use).astype(jnp.float32)
            terms = (
                jnp.einsum("rij,sri->srj", tile_now, row_values, precision=highest)
                * live[None, :, None]
            )
            placing = (slot_cols[:, None] == group_ids[None, :]).astype(jnp.float32)
            return total + jnp.einsum("rc,srj->scj", placing, terms, precision=highest)

        start = jnp.zeros((scenarios, groups, width), jnp.float32)
        total = lax.fori_loop(jnp.int32(0), longest, backward_add_slot, start)
        return total.reshape(scenarios, groups * width)

    primal = jnp.zeros((scenarios, groups * width), jnp.float32)
    dual_now = jnp.zeros((scenarios, row_blocks * width), jnp.float32)
    weight = primal_weight
    for iteration in range(ITERS):
        primal_step = (step_size / weight)[:, None]
        dual_step = (step_size * weight)[:, None]
        if iteration == 0:
            dual_image = jnp.zeros((scenarios, groups * width), jnp.float32)
        else:
            dual_image = lax.psum(backward(dual_now), "rows")
        new_primal = project_primal(
            primal - primal_step * (objective[None, :] - dual_image),
            var_kind,
            lower_bound,
            upper_bound,
        )
        primal_part = jnp.sum((new_primal - primal) ** 2, axis=1)
        primal_image = lax.psum(forward(2.0 * new_primal - primal), "cols")
        new_dual = project_dual(dual_now + dual_step * (demand - primal_image), row_kind)
        dual_part = jnp.sum((new_dual - dual_now) ** 2, axis=1)
        dual_move = lax.psum(dual_part, "rows")
        primal_move = lax.psum(primal_part, "cols")
        weight = jnp.sqrt(weight * jnp.sqrt((dual_move + epsilon) / (primal_move + epsilon)))
        primal = new_primal
        dual_now = new_dual
    return (primal, dual_now, weight)


def solution(mesh):
    return jax.shard_map(
        local,
        mesh=mesh,
        in_specs=(
            P("rows", "cols", None, None, None),
            P("rows", "cols", None),
            P("rows", "cols"),
            P("cols"),
            P("cols"),
            P("cols"),
            P("cols"),
            P(None, "rows"),
            P("rows"),
            P(),
            P(),
        ),
        out_specs=(P(None, "cols"), P(None, "rows"), P()),
        check_vma=False,
    )
```

profile of v0, /device:TPU:0, one launch (start us, length us, event | category | flops | bytes accessed | tf_op | source)
XLA Modules:
  0.0 654.5 jit_solution(3972520806985442484)
XLA Ops:
  7.3 4.7 copy.33
  12.8 49.4 %while.77 = (s32[]{:T(128)}, f32[32,4,128]{2,0,1:T(8,128)S(1)}, s32[]{:T(128)}, s32[4,16]{0,1:T(8,128)S(1)}, s32[4]{0:T(128)S(1)}, /*index=5*/f32[4,16,128,128]{...) while((s32[]{:T(128)}, f32[32,4,128]{2,0,1:T(8,128)S(1)}, ...), condition=%wide.region_2.4_spmd.clone, body=%wide.region_1.0_spmd.clone.sunk | while | flops 26133540 | bytes 1175987 | solution.py:59
  62.9 36.2 %all-reduce.8.cloned.1.call-done = f32[32,512]{1,0:T(8,128)} async-done(((f32[32,512]{1,0:T(8,128)}), f32[32,512]{1,0:T(8,128)}) %all-reduce.8.cloned.1.call-update) | async-done | bytes 65552 | tf_op jit(solution)/shard_map/psum | solution.py:97
  100.3 41.7 %while.78 = (s32[]{:T(128)}, f32[32,32,128]{2,1,0:T(8,128)S(1)}, s32[]{:T(128)}, f32[4,16,128,128]{3,2,1,0:T(8,128)}, f32[32,4,128]{2,1,0:T(4,128)S(1)}, /*index...) while((s32[]{:T(128)}, f32[32,32,128]{2,1,0:T(8,128)S(1)}, ...), condition=%wide.region_9.11_spmd.clone, body=%wide.region_8.10_spmd.clone.sunk | while | flops 31604876 | bytes 1507571 | solution.py:77
  143.5 10.5 %psum.107 = f32[32]{0:T(128)S(1)} all-reduce(f32[32]{0:T(128)S(1)} %multiply_reduce_fusion.3), channel_id=1, replica_groups=mesh['rows'=8,'cols'=4] {'cols'}, use_global_device_ids=true, to_apply=%region_7.9 | all-reduce | flops 32 | bytes 256 | tf_op jit(solution)/shard_map/psum | solution.py:101
  154.0 11.8 %psum.106 = f32[32]{0:T(128)S(1)} all-reduce(f32[32]{0:T(128)S(1)} %get-tuple-element.616), channel_id=1, replica_groups=mesh['rows'=8,'cols'=4] {'rows'}, use_global_device_ids=true, to_apply=%region_5.7 | all-reduce | flops 32 | bytes 256 | tf_op jit(solution)/shard_map/psum | solution.py:100
  165.8 30.8 %all-reduce.10.cloned.1.call-done = f32[32,4096]{1,0:T(8,128)} async-done(((f32[32,4096]{1,0:T(8,128)}), f32[32,4096]{1,0:T(8,128)}) %all-reduce.10.cloned.1.call-update) | async-done | bytes 524304 | tf_op jit(solution)/shard_map/psum | solution.py:89
  198.2 45.2 %while.74 = (s32[]{:T(128)}, f32[32,4,128]{2,0,1:T(8,128)S(1)}, s32[]{:T(128)}, s32[4,16]{0,1:T(8,128)S(1)}, f32[32,32,128]{2,0,1:T(8,128)S(1)}, /*index=5*/s32[...) while((s32[]{:T(128)}, f32[32,4,128]{2,0,1:T(8,128)S(1)}, s32[]{:T(128)}, ...), condition=%wide.region_12.14_spmd, body=%wide.region_11.13_spmd.sunk | while | flops 25216036 | bytes 594187 | solution.py:59
  244.1 33.1 %all-reduce.12.cloned.1.call-done = f32[32,512]{1,0:T(8,128)} async-done(((f32[32,512]{1,0:T(8,128)}), f32[32,512]{1,0:T(8,128)}) %all-reduce.12.cloned.1.call-update) | async-done | bytes 65552 | tf_op jit(solution)/shard_map/psum | solution.py:97
  278.3 41.7 %while.79 = (s32[]{:T(128)}, f32[32,32,128]{2,1,0:T(8,128)S(1)}, s32[]{:T(128)}, f32[4,16,128,128]{3,2,1,0:T(8,128)}, f32[32,4,128]{2,1,0:T(4,128)S(1)}, /*index...) while((s32[]{:T(128)}, f32[32,32,128]{2,1,0:T(8,128)S(1)}, ...), condition=%wide.region_19.21_spmd.clone, body=%wide.region_18.20_spmd.clone.sunk | while | flops 31604876 | bytes 1507571 | solution.py:77
  321.2 10.5 %psum.111 = f32[32]{0:T(128)S(1)} all-reduce(f32[32]{0:T(128)S(1)} %get-tuple-element.622), channel_id=1, replica_groups=mesh['rows'=8,'cols'=4] {'cols'}, use_global_device_ids=true, to_apply=%region_17.19 | all-reduce | flops 32 | bytes 256 | tf_op jit(solution)/shard_map/psum | solution.py:101
  331.7 11.9 %psum.110 = f32[32]{0:T(128)S(1)} all-reduce(f32[32]{0:T(128)S(1)} %get-tuple-element.612), channel_id=1, replica_groups=mesh['rows'=8,'cols'=4] {'rows'}, use_global_device_ids=true, to_apply=%region_15.17 | all-reduce | flops 32 | bytes 256 | tf_op jit(solution)/shard_map/psum | solution.py:100
  343.6 31.1 %all-reduce.14.cloned.1.call-done = f32[32,4096]{1,0:T(8,128)} async-done(((f32[32,4096]{1,0:T(8,128)}), f32[32,4096]{1,0:T(8,128)}) %all-reduce.14.cloned.1.call-update) | async-done | bytes 524304 | tf_op jit(solution)/shard_map/psum | solution.py:89
  376.8 45.1 %while.75 = (s32[]{:T(128)}, f32[32,4,128]{2,0,1:T(8,128)S(1)}, s32[]{:T(128)}, s32[4,16]{0,1:T(8,128)S(1)}, f32[32,32,128]{2,0,1:T(8,128)S(1)}, /*index=5*/s32[...) while((s32[]{:T(128)}, f32[32,4,128]{2,0,1:T(8,128)S(1)}, s32[]{:T(128)}, ...), condition=%wide.region_22.24_spmd, body=%wide.region_21.23_spmd.sunk | while | flops 25216036 | bytes 594187 | solution.py:59
  422.6 33.1 %all-reduce.16.cloned.1.call-done = f32[32,512]{1,0:T(8,128)} async-done(((f32[32,512]{1,0:T(8,128)}), f32[32,512]{1,0:T(8,128)}) %all-reduce.16.cloned.1.call-update) | async-done | bytes 65552 | tf_op jit(solution)/shard_map/psum | solution.py:97
  456.8 41.7 %while.80 = (s32[]{:T(128)}, f32[32,32,128]{2,1,0:T(8,128)S(1)}, s32[]{:T(128)}, f32[4,16,128,128]{3,2,1,0:T(8,128)}, f32[32,4,128]{2,1,0:T(4,128)S(1)}, /*index...) while((s32[]{:T(128)}, f32[32,32,128]{2,1,0:T(8,128)S(1)}, ...), condition=%wide.region_29.31_spmd.clone, body=%wide.region_28.30_spmd.clone.sunk | while | flops 31604876 | bytes 1507571 | solution.py:77
  499.7 10.5 %psum.115 = f32[32]{0:T(128)S(1)} all-reduce(f32[32]{0:T(128)S(1)} %get-tuple-element.608), channel_id=1, replica_groups=mesh['rows'=8,'cols'=4] {'cols'}, use_global_device_ids=true, to_apply=%region_27.29 | all-reduce | flops 32 | bytes 256 | tf_op jit(solution)/shard_map/psum | solution.py:101
  510.2 11.9 %psum.114 = f32[32]{0:T(128)S(1)} all-reduce(f32[32]{0:T(128)S(1)} %get-tuple-element.606), channel_id=1, replica_groups=mesh['rows'=8,'cols'=4] {'rows'}, use_global_device_ids=true, to_apply=%region_25.27 | all-reduce | flops 32 | bytes 256 | tf_op jit(solution)/shard_map/psum | solution.py:100
  522.1 31.1 %all-reduce.18.cloned.1.call-done = f32[32,4096]{1,0:T(8,128)} async-done(((f32[32,4096]{1,0:T(8,128)}), f32[32,4096]{1,0:T(8,128)}) %all-reduce.18.cloned.1.call-update) | async-done | bytes 524304 | tf_op jit(solution)/shard_map/psum | solution.py:89
  554.7 45.1 %while.76 = (s32[]{:T(128)}, f32[32,4,128]{2,0,1:T(8,128)S(1)}, s32[]{:T(128)}, s32[4,16]{0,1:T(8,128)S(1)}, f32[32,32,128]{2,0,1:T(8,128)S(1)}, /*index=5*/s32[...) while((s32[]{:T(128)}, f32[32,4,128]{2,0,1:T(8,128)S(1)}, s32[]{:T(128)}, ...), condition=%wide.region_32.34_spmd, body=%wide.region_31.33_spmd.sunk | while | flops 25216036 | bytes 594187 | solution.py:59
  600.5 11.6 %psum.119 = f32[32]{0:T(128)S(1)} all-reduce(f32[32]{0:T(128)S(1)} %get-tuple-element.602), channel_id=1, replica_groups=mesh['rows'=8,'cols'=4] {'cols'}, use_global_device_ids=true, to_apply=%region_37.39 | all-reduce | flops 32 | bytes 256 | tf_op jit(solution)/shard_map/psum | solution.py:101
  612.1 21.5 %all-reduce.20.cloned.1.call-done = f32[32,512]{1,0:T(8,128)} async-done(((f32[32,512]{1,0:T(8,128)}), f32[32,512]{1,0:T(8,128)}) %all-reduce.20.cloned.1.call-update) | async-done | bytes 65552 | tf_op jit(solution)/shard_map/psum | solution.py:97
  633.6 1.7 multiply_reduce_fusion.4
  635.3 11.8 %psum.118 = f32[32]{0:T(128)S(1)} all-reduce(f32[32]{0:T(128)S(1)} %get-tuple-element.600), channel_id=1, replica_groups=mesh['rows'=8,'cols'=4] {'rows'}, use_global_device_ids=true, to_apply=%region_35.37 | all-reduce | flops 32 | bytes 256 | tf_op jit(solution)/shard_map/psum | solution.py:100
  (541 shorter events, 245.8 us)
Async XLA Ops:
  7.2 92.0 %all-reduce.8.cloned.1.call-start = ((), (), s32[]{:S(2)}) async-start(), calls=%async_computation | async-start | bytes 131072 | tf_op jit(solution)/shard_map/psum | solution.py:97
  7.2 4.7 copy-start.7
  7.2 4.7 copy-start.9
  7.2 4.8 copy-start.6
  7.2 5.5 copy-start.8
  7.3 5.5 copy-start.11
  7.3 5.5 copy-start.2
  7.3 5.5 copy-start.3
  7.3 5.5 copy-start.4
  12.0 50.9 %copy-start.10 = (s32[512]{0:T(512)S(1)}, s32[512]{0:T(512)}, u32[]{:S(2)}) copy-start(s32[512]{0:T(512)} %param.35) | copy-start | bytes 6148
  12.0 87.2 %copy-start.5 = (f32[32,512]{1,0:T(8,128)S(1)}, f32[32,512]{1,0:T(8,128)}, u32[]{:S(2)}) copy-start(f32[32,512]{1,0:T(8,128)} %param.34) | copy-start | bytes 196612
  62.8 133.7 %all-reduce.10.cloned.1.call-start = ((), (), s32[]{:S(2)}) async-start(), calls=%async_computation.1 | async-start | bytes 1048576 | tf_op jit(solution)/shard_map/psum | solution.py:89
  143.1 134.1 %all-reduce.12.cloned.1.call-start = ((), (), s32[]{:S(2)}) async-start(), calls=%async_computation.2 | async-start | bytes 131072 | tf_op jit(solution)/shard_map/psum | solution.py:97
  244.0 130.7 %all-reduce.14.cloned.1.call-start = ((), (), s32[]{:S(2)}) async-start(), calls=%async_computation.3 | async-start | bytes 1048576 | tf_op jit(solution)/shard_map/psum | solution.py:89
  278.3 96.4 %copy-start = (f32[32,4096]{1,0:T(8,128)S(1)}, f32[32,4096]{1,0:T(8,128)}, u32[]{:S(2)}) copy-start(f32[32,4096]{1,0:T(8,128)} %all-reduce.10.cloned.1.call-done) | copy-start | bytes 1572868
  321.2 134.5 %all-reduce.16.cloned.1.call-start = ((), (), s32[]{:S(2)}) async-start(), calls=%async_computation.4 | async-start | bytes 131072 | tf_op jit(solution)/shard_map/psum | solution.py:97
  422.6 130.6 %all-reduce.18.cloned.1.call-start = ((), (), s32[]{:S(2)}) async-start(), calls=%async_computation.5 | async-start | bytes 1048576 | tf_op jit(solution)/shard_map/psum | solution.py:89
  499.6 134.0 %all-reduce.20.cloned.1.call-start = ((), (), s32[]{:S(2)}) async-start(), calls=%async_computation.6 | async-start | bytes 131072 | tf_op jit(solution)/shard_map/psum | solution.py:97
  554.6 93.1 %copy-start.1 = (f32[32,4096]{1,0:T(8,128)}, f32[32,4096]{1,0:T(8,128)S(1)}, u32[]{:S(2)}) copy-start(f32[32,4096]{1,0:T(8,128)S(1)} %get-tuple-element.603) | copy-start | bytes 1572868
Sparse Core Ops, SparseCore 0:
  62.9 36.1 all-reduce.7
  143.2 53.3 all-reduce.9
  244.2 32.9 all-reduce.11
  321.3 53.3 all-reduce.13
  422.7 32.9 all-reduce.15
  499.8 53.3 all-reduce.17
  600.6 32.9 all-reduce.19
where the time goes:
time: 662 us; the launch traced here: 654 us
  waiting for transfers between devices  217 us (33%)
  matrix products  188 us (28%)
  blocking collectives  90.4 us (14%)
  loops' own time  80.6 us (12%)
  local copies, waits for them, and re-layouts  46.6 us (7%)
  other arithmetic  17.2 us (3%)
  between operations  14.5 us (2%)
    psum x4, waiting for transfers between devices, local(): primal_image = lax.psum(forward(2.0 * new_primal - primal), 'cols')  124 us
    dot_general x64, matrix products, forward_add_slot(): jnp.einsum('rij,srj->sri', tile_now, taken, precision=highest)  97.6 us
    psum x3, waiting for transfers between devices, local(): dual_image = lax.psum(backward(dual_now), 'rows')  93 us
    dot_general x48, matrix products, backward_add_slot(): jnp.einsum('rij,sri->srj', tile_now, row_values, precision=highest)  62.5 us
    psum x4, blocking collectives, local(): dual_move = lax.psum(dual_part, 'rows')  47.4 us
    another operation x4, loops' own time, forward(): total = lax.fori_loop(jnp.int32(0), longest, forward_add_slot, start)  46.3 us
    psum x4, blocking collectives, local(): primal_move = lax.psum(primal_part, 'cols')  43 us
    gather x64, local copies, waits for them, and re-layouts, forward_add_slot(): taken = jnp.take(field_blocks, slot_cols, axis=1) * live[None, :, None]  35.4 us
  transfers between devices with their start and end apart: 7, of which 7 were waited for; matrix products, arithmetic and copies ran while one was open for 0% of the time, Pallas kernels for 0%

commit v1 on v0

v1 whole, which is shorter than its diff:
```python
import functools

import jax
import jax.numpy as jnp
from jax import lax
from jax.experimental import pallas as pl
from jax.experimental.pallas import tpu as pltpu
from jax.sharding import PartitionSpec as P

ITERS = 4
EPS = 1e-06
LANES = 128
MESH = pl.DeviceIdType.MESH
f32 = jnp.float32
bf16 = jnp.bfloat16


def split(values):
    high = values.astype(bf16)
    low = (values - high.astype(f32)).astype(bf16)
    return high, low


def matmul(left, right, transposed):
    dims = (((1,), (1 if transposed else 0,)), ((), ()))
    return lax.dot_general(left, right, dims, preferred_element_type=f32)


def kernel(
    R,
    C,
    slot_ref,
    blocks_ref,
    obj_ref,
    lb_ref,
    ub_ref,
    vk_ref,
    demand_ref,
    rk_ref,
    step_ref,
    pw_ref,
    x_ref,
    u_ref,
    w_ref,
    k_hi,
    k_lo,
    a_src,
    a_dst,
    b_src,
    b_dst,
    x_new,
    x_old,
    d_src,
    d_dst,
    e_buf,
    n_buf,
    steps,
    weights,
    a_sem,
    b_sem,
    c_sem,
    f_sem,
    d_sem,
    e_sem,
    n_sem,
):
    me = lax.axis_index("rows")
    col = lax.axis_index("cols")
    core = lax.rem(me, 2)
    chip = lax.div(me, 2)
    sibling = me + 1 - 2 * core
    chips = R // 2
    row_blocks, width = blocks_ref.shape[0], blocks_ref.shape[2]
    rows = row_blocks * width
    S = x_ref.shape[0]
    part = S // C
    chunk = x_new.shape[2]
    tiles = chunk // width
    group = LANES // C

    barrier = pltpu.get_barrier_semaphore()
    for o in range(1, R):
        pl.semaphore_signal(barrier, inc=1, device_id={"rows": lax.rem(me + o, R)}, device_id_type=MESH)
    for o in range(1, C):
        pl.semaphore_signal(barrier, inc=1, device_id={"cols": lax.rem(col + o, C)}, device_id_type=MESH)

    def copy(src, dst, sem, o, axis, target):
        return pltpu.make_async_remote_copy(
            src_ref=src,
            dst_ref=dst,
            send_sem=sem.at[0, o],
            recv_sem=sem.at[1, o],
            device_id={axis: target},
            device_id_type=MESH,
        )

    def chip_at(o):
        return lax.rem(chip + o, chips)

    def chip_from(o):
        return lax.rem(chip + chips - o, chips)

    eye = lax.broadcasted_iota(jnp.int32, (S, S), 0) == lax.broadcasted_iota(jnp.int32, (S, S), 1)

    def upright(ref):
        return jnp.sum(jnp.where(eye, jnp.broadcast_to(ref[...], (S, S)), 0.0), axis=1, keepdims=True)

    step_all = upright(step_ref)
    weight_all = upright(pw_ref)
    for k in range(C):
        rows_k = slice(k * part, (k + 1) * part)
        steps[k] = jnp.broadcast_to(step_all[rows_k], (part, LANES))
        weights[k] = jnp.broadcast_to(weight_all[rows_k], (part, LANES))

    def stacked(ref):
        return jnp.concatenate([ref[k] for k in range(C)], axis=0)

    def project(values, at):
        lb, ub, kind = lb_ref[:, at], ub_ref[:, at], vk_ref[:, at]
        floored = jnp.maximum(values, lb)
        boxed = jnp.minimum(floored, ub)
        return jnp.where(kind == 0, values, jnp.where(kind == 1, floored, boxed))

    def columns(q):
        return pl.ds(pl.multiple_of(q * chunk, LANES), chunk)

    def forward(field, q):
        high, low = split(field)
        both = matmul(jnp.concatenate([high, low], axis=0), k_hi[q], True)
        return both[:S] + both[S:] + matmul(high, k_lo[q], True)

    def cols_phase(total, primal_part, old_dual):
        moved = jnp.broadcast_to(primal_part, (S, LANES))
        for k in range(C):
            rows_k = slice(k * part, (k + 1) * part)
            d_src[k, :, :rows] = total[rows_k]
            d_src[k, :, rows:] = moved[rows_k]
        sends = []
        for o in range(1, C):
            target = lax.rem(col + o, C)
            c = copy(d_src.at[target], d_dst.at[col], d_sem, o, "cols", target)
            c.start()
            sends.append(c)
        image = d_src[col]
        for o in range(1, C):
            source = lax.rem(col + C - o, C)
            copy(d_src.at[source], d_dst.at[source], d_sem, o, "cols", source).wait_recv()
            image = image + d_dst[source]
        sigma = (steps[col] * weights[col])[:, :1]
        fresh = old_dual + sigma * (demand_ref[col] - image[:, :rows])
        fresh = jnp.where(rk_ref[...] == 1, jnp.maximum(fresh, 0.0), fresh)
        dual_part = jnp.sum((fresh - old_dual) ** 2, axis=1, keepdims=True)
        lane = lax.broadcasted_iota(jnp.int32, (part, LANES), 1)
        e_buf[col, :, :rows] = fresh
        e_buf[col, :, rows:] = jnp.where(lane < LANES // 2, image[:, rows:], dual_part)
        for o in range(1, C):
            target = lax.rem(col + o, C)
            c = copy(e_buf.at[col], e_buf.at[col], e_sem, o, "cols", target)
            c.start()
            sends.append(c)
        for o in range(1, C):
            source = lax.rem(col + C - o, C)
            copy(e_buf.at[source], e_buf.at[source], e_sem, o, "cols", source).wait_recv()
        norms = jnp.zeros((part, LANES), f32)
        for k in range(C):
            moves = e_buf[k, :, rows:]
            pair = jnp.where(lax.rem(lane, group) < group // 2, moves[:, :1], moves[:, LANES // 2 : LANES // 2 + 1])
            norms = jnp.where(lax.div(lane, group) == k, pair, norms)
        n_buf[me] = norms
        for o in range(1, R):
            copy(n_buf.at[me], n_buf.at[me], n_sem, o, "rows", lax.rem(me + o, R)).start()
        for c in sends:
            c.wait_send()

    def take_norms():
        for o in range(1, R):
            source = lax.rem(me + R - o, R)
            copy(n_buf.at[source], n_buf.at[source], n_sem, o, "rows", source).wait_recv()
        norms = n_buf[0]
        for r in range(1, R):
            norms = norms + n_buf[r]
        for k in range(C):
            primal_move = norms[:, k * group : k * group + 1]
            dual_move = norms[:, k * group + group // 2 : k * group + group // 2 + 1]
            ratio = (dual_move + EPS) / (primal_move + EPS)
            weights[k] = jnp.sqrt(weights[k] * jnp.sqrt(ratio))
        for o in range(1, R):
            copy(n_buf.at[me], n_buf.at[me], n_sem, o, "rows", lax.rem(me + o, R)).wait_send()

    tau = (stacked(steps) / stacked(weights))[:, :1]

    def first(q, total):
        for r in range(row_blocks):
            for t in range(tiles):
                slot = slot_ref[r, q * tiles + t]
                tile = blocks_ref[r, jnp.maximum(slot, 0)]
                tile = jnp.where(slot >= 0, tile, 0.0)
                high, low = split(tile)
                k_hi[q, r * width : (r + 1) * width, t * width : (t + 1) * width] = high
                k_lo[q, r * width : (r + 1) * width, t * width : (t + 1) * width] = low
        at = columns(q)
        fresh = project(-tau * obj_ref[:, at], at)
        x_old[q] = fresh
        return total + forward(2.0 * fresh, q)

    total = lax.fori_loop(0, R, first, jnp.zeros((S, rows), f32))
    pl.semaphore_wait(barrier, R + C - 2)
    own = x_old[me]
    cols_phase(total, jnp.sum(own * own, axis=1, keepdims=True), jnp.zeros((part, rows), f32))

    def iteration(step, carry):
        dual = jnp.concatenate([e_buf[k, :, :rows] for k in range(C)], axis=0)
        dual_hi, dual_lo = split(dual)
        dual_both = jnp.concatenate([dual_hi, dual_lo], axis=0)

        def backward(q):
            both = matmul(dual_both, k_hi[q], False)
            return both[:S] + both[S:] + matmul(dual_hi, k_lo[q], False)

        sends = []
        order = list(range(1, chips)) + [0]
        for o in order:
            p = chip_at(o)
            a_src[o] = backward(2 * p + 1 - core)
            c = copy(a_src.at[o], a_dst.at[p], a_sem, o, "rows", sibling)
            c.start()
            sends.append(c)
        for o in order:
            p = chip_at(o)
            mine = backward(2 * p + core)
            copy(a_src.at[o], a_dst.at[p], a_sem, o, "rows", sibling).wait_recv()
            mine = mine + a_dst[p]
            if o > 0:
                b_src[o] = mine
                c = copy(b_src.at[o], b_dst.at[o], b_sem, o, "rows", 2 * p + core)
                c.start()
                sends.append(c)
        take_norms()
        tau = (stacked(steps) / stacked(weights))[:, :1]
        image = mine
        for o in range(1, chips):
            copy(b_src.at[o], b_dst.at[o], b_sem, o, "rows", 2 * chip_at(o) + core).wait_recv()
            image = image + b_dst[o]
        at = columns(me)
        before = x_old[me]
        fresh = project(before - tau * (obj_ref[:, at] - image), at)
        x_new[me] = fresh
        for o in range(1, chips):
            c = copy(x_new.at[me], x_new.at[me], c_sem, o, "rows", 2 * chip_at(o) + core)
            c.start()
            sends.append(c)
        c = copy(x_new.at[me], x_new.at[me], c_sem, 0, "rows", sibling)
        c.start()
        sends.append(c)
        primal_part = jnp.sum((fresh - before) ** 2, axis=1, keepdims=True)
        x_old[me] = fresh
        total = forward(2.0 * fresh - before, me)

        def add(q, total):
            now = x_new[q]
            field = 2.0 * now - x_old[q]
            x_old[q] = now
            return total + forward(field, q)

        copy(x_new.at[sibling], x_new.at[sibling], c_sem, 0, "rows", sibling).wait_recv()
        total = add(sibling, total)
        for o in range(1, chips):
            q = 2 * chip_from(o) + core
            copy(x_new.at[q], x_new.at[q], c_sem, o, "rows", q).wait_recv()
            c = copy(x_new.at[q], x_new.at[q], f_sem, o, "rows", sibling)
            c.start()
            sends.append(c)
            total = add(q, total)
        for o in range(1, chips):
            q = 2 * chip_from(o) + 1 - core
            copy(x_new.at[q], x_new.at[q], f_sem, o, "rows", sibling).wait_recv()
            total = add(q, total)
        for c in sends:
            c.wait_send()
        cols_phase(total, primal_part, e_buf[col, :, :rows])
        return carry

    lax.fori_loop(1, ITERS, iteration, 0)
    take_norms()
    for q in range(R):
        x_ref[:, q * chunk : (q + 1) * chunk] = x_old[q]
    u_ref[...] = jnp.concatenate([e_buf[k, :, :rows] for k in range(C)], axis=0)
    final = jnp.broadcast_to(stacked(weights)[:, :1], (S, S))
    w_ref[...] = jnp.sum(jnp.where(eye, final, 0.0), axis=0, keepdims=True)


def solution(mesh):
    R, C = mesh.shape["rows"], mesh.shape["cols"]

    def local(blocks, ell_index, counts, objective, lower, upper, var_kind, demand, row_kind, step_size, primal_weight):
        row_blocks, _, slots, width, _ = blocks.shape
        n_vars = objective.shape[0]
        S, rows = demand.shape
        part, chunk = S // C, n_vars // R
        groups = n_vars // width
        ids = ell_index.reshape(row_blocks, slots)
        used = jnp.arange(slots, dtype=jnp.int32)[None, :] < counts.reshape(row_blocks, 1)
        hit = (ids[:, None, :] == jnp.arange(groups, dtype=jnp.int32)[None, :, None]) & used[:, None, :]
        slot_of = jnp.sum(jnp.where(hit, jnp.arange(1, slots + 1, dtype=jnp.int32)[None, None, :], 0), axis=2) - 1
        vmem = pl.BlockSpec(memory_space=pltpu.VMEM)
        primal, dual, weight = pl.pallas_call(
            functools.partial(kernel, R, C),
            out_shape=(
                jax.ShapeDtypeStruct((S, n_vars), f32),
                jax.ShapeDtypeStruct((S, rows), f32),
                jax.ShapeDtypeStruct((1, S), f32),
            ),
            in_specs=[pl.BlockSpec(memory_space=pltpu.SMEM)] + [vmem] * 9,
            out_specs=(vmem, vmem, vmem),
            scratch_shapes=[
                pltpu.VMEM((R, rows, chunk), bf16),
                pltpu.VMEM((R, rows, chunk), bf16),
                pltpu.VMEM((R // 2, S, chunk), f32),
                pltpu.VMEM((R // 2, S, chunk), f32),
                pltpu.VMEM((R // 2, S, chunk), f32),
                pltpu.VMEM((R // 2, S, chunk), f32),
                pltpu.VMEM((R, S, chunk), f32),
                pltpu.VMEM((R, S, chunk), f32),
                pltpu.VMEM((C, part, rows + LANES), f32),
                pltpu.VMEM((C, part, rows + LANES), f32),
                pltpu.VMEM((C, part, rows + LANES), f32),
                pltpu.VMEM((R, part, LANES), f32),
                pltpu.VMEM((C, part, LANES), f32),
                pltpu.VMEM((C, part, LANES), f32),
                pltpu.SemaphoreType.DMA((2, R // 2)),
                pltpu.SemaphoreType.DMA((2, R // 2)),
                pltpu.SemaphoreType.DMA((2, R // 2)),
                pltpu.SemaphoreType.DMA((2, R // 2)),
                pltpu.SemaphoreType.DMA((2, C)),
                pltpu.SemaphoreType.DMA((2, C)),
                pltpu.SemaphoreType.DMA((2, R)),
            ],
            compiler_params=pltpu.CompilerParams(
                collective_id=0, has_side_effects=True, vmem_limit_bytes=48 * 1024 * 1024
            ),
        )(
            slot_of,
            blocks.reshape(row_blocks, slots, width, width),
            objective.reshape(1, n_vars),
            lower.reshape(1, n_vars),
            upper.reshape(1, n_vars),
            var_kind.reshape(1, n_vars),
            demand.reshape(C, part, rows),
            row_kind.reshape(1, rows),
            step_size.reshape(1, S),
            primal_weight.reshape(1, S),
        )
        return primal, dual, weight.reshape(S)

    return jax.shard_map(
        local,
        mesh=mesh,
        in_specs=(
            P("rows", "cols", None, None, None),
            P("rows", "cols", None),
            P("rows", "cols"),
            P("cols"),
            P("cols"),
            P("cols"),
            P("cols"),
            P(None, "rows"),
            P("rows"),
            P(),
            P(),
        ),
        out_specs=(P(None, "cols"), P(None, "rows"), P()),
        check_vma=False,
    )
```

time: 662 us -> 96.2 us (0.15); the launches traced: 654 us -> 95.6 us
  waiting for transfers between devices: 217 us -> 0 us
  matrix products: 188 us -> 0 us
  blocking collectives: 90.4 us -> 0 us
  Pallas kernels: 0 us -> 83.6 us
  loops' own time: 80.6 us -> 0 us
  local copies, waits for them, and re-layouts: 46.6 us -> 9.82 us
  other arithmetic: 17.2 us -> 1.51 us
  between operations: 14.5 us -> 0.67 us
    psum x7 -> x0, waiting for transfers between devices: 217 us -> none  [the longest x4 124 us: local(): primal_image = lax.psum(forward(2.0 * new_primal - primal), 'cols')]
    dot_general x160 -> x0, matrix products: 188 us -> none  [the longest x64 97.6 us: forward_add_slot(): jnp.einsum('rij,srj->sri', tile_now, taken, precision=highest)]
    psum x8 -> x0, blocking collectives: 90.4 us -> none  [the longest x4 47.4 us: local(): dual_move = lax.psum(dual_part, 'rows')]
    pallas_call x0 -> x1, Pallas kernels: none -> 83.6 us  [local(): pl.pallas_call(functools.partial(kernel, R, C), out_shape=(jax.ShapeDtype...]
    another operation x7 -> x0, loops' own time: 80.6 us -> none  [the longest x4 46.3 us: forward(): total = lax.fori_loop(jnp.int32(0), longest, forward_add_slot, start)]
    gather x64 -> x0, local copies, waits for them, and re-layouts: 35.4 us -> none  [forward_add_slot(): taken = jnp.take(field_blocks, slot_cols, axis=1) * live[None, :, None]]
    reduce_sum x8 -> x1, other arithmetic: 9.68 us -> 0.78 us  [local(): jnp.sum(jnp.where(hit, jnp.arange(1, slots + 1, dtype=jnp.int32)[None, No...]
  transfers between devices with their start and end apart: 7 -> 0, of which waited for: 7 -> 0; matrix products, arithmetic and copies ran while one was open for 0% -> 0% of each run, Pallas kernels for 0% -> 0%
where the time goes in v1:
time: 96.2 us; the launch traced here: 95.6 us
  Pallas kernels  83.6 us (87%)
  local copies, waits for them, and re-layouts  9.82 us (10%)
  other arithmetic  1.51 us (2%)
    pallas_call x1, Pallas kernels, local(): pl.pallas_call(functools.partial(kernel, R, C), out_shape=(jax.ShapeDtype...  83.6 us
    unnamed x21, local copies, waits for them, and re-layouts  9.82 us

profile of v1, /device:TPU:0, one launch (start us, length us, event | category | flops | bytes accessed | tf_op | source)
XLA Modules:
  0.0 95.6 jit_solution(6604136052511473069)
XLA Ops:
  0.6 0.7 iota_compare_fusion.1
  1.4 0.8 select_reduce_fusion
  2.2 0.0 copy-start
  2.2 2.2 %copy-done = f32[4,1,16,128,128]{4,3,2,1,0:T(8,128)S(1)} copy-done((f32[4,1,16,128,128]{4,3,2,1,0:T(8,128)S(1)}, f32[4,1,16,128,128]{4,3,2,1,0:T(8,128)}, u32[]{:S(2)}) %copy-start) | copy-done | bytes 4194328
  4.3 0.0 copy-start.1
  4.3 0.8 copy-done.1
  5.2 0.0 copy-start.2
  5.2 0.7 copy-done.2
  5.9 0.0 copy-start.3
  5.9 0.7 copy-done.3
  6.6 0.0 copy-start.4
  6.6 0.7 copy-done.4
  7.3 0.0 copy-start.5
  7.3 0.7 copy-done.5
  8.1 0.0 copy-start.6
  8.1 0.7 copy-done.6
  8.7 0.0 copy-start.7
  8.7 0.7 copy-done.7
  9.4 0.0 copy-start.8
  9.4 0.7 copy-done.8
  10.0 83.6 %shard_map.130 = (f32[32,4096]{1,0:T(8,128)S(1)}, f32[32,512]{1,0:T(8,128)S(1)}, f32[1,32]{1,0:T(1,128)S(1)}) custom-call(s32[4,32]{1,0:T(4,128)S(1)} %broadcast_add_fusion.slot_ref, f32[4,16,128,128]{3,2,1,0:T(8,128)S(1)} %bitcast.12, f32[1,4096]{1,0:T(1,128)S(1)} %bitcast.14, f32[1,4096]{1,0:T(1,128)S(1)} %bitcast.15, f32[1,4096]{1,0:T(1,128)S(1)} %bitcast.16, ...), custom_call_target="tpu_custom_call" | custom-call | tf_op jit(solution)/shard_map/pallas_call | solution.py:306
  93.7 0.8 copy.17
  94.5 0.6 copy.18
  95.1 0.5 copy.19
  (2 shorter events, 0.0 us)
Async XLA Ops:
  2.2 2.2 %copy-start = (f32[4,1,16,128,128]{4,3,2,1,0:T(8,128)S(1)}, f32[4,1,16,128,128]{4,3,2,1,0:T(8,128)}, u32[]{:S(2)}) copy-start(f32[4,1,16,128,128]{4,3,2,1,0:T(8,128)} %param.11) | copy-start | bytes 12582916
  4.3 0.8 copy-start.1
  5.2 0.7 copy-start.2
  5.9 0.7 copy-start.3
  6.6 0.7 copy-start.4
  7.3 0.7 copy-start.5
  8.1 0.7 copy-start.6
  8.7 0.7 copy-start.7
  9.4 0.7 copy-start.8

commit v2 on v1

v2 whole, which is shorter than its diff:
```python
import functools

import jax
import jax.numpy as jnp
from jax import lax
from jax.experimental import pallas as pl
from jax.experimental.pallas import tpu as pltpu
from jax.sharding import PartitionSpec as P

ITERS = 4
HALVES = 2
SUB = 8
EPS = 1e-06
LANES = 128
MESH = pl.DeviceIdType.MESH
f32 = jnp.float32
bf16 = jnp.bfloat16


def split(values):
    high = values.astype(bf16)
    low = (values - high.astype(f32)).astype(bf16)
    return high, low


def matmul(left, right, transposed):
    dims = (((1,), (1 if transposed else 0,)), ((), ()))
    return lax.dot_general(left, right, dims, preferred_element_type=f32)


def kernel(
    R,
    C,
    blocks_hbm,
    ids_hbm,
    counts_hbm,
    obj_hbm,
    lb_hbm,
    ub_hbm,
    vk_hbm,
    demand_hbm,
    rk_hbm,
    step_hbm,
    pw_hbm,
    x_hbm,
    u_hbm,
    w_ref,
    blocks_ref,
    ids_ref,
    counts_ref,
    obj_ref,
    lb_ref,
    ub_ref,
    vk_ref,
    demand_ref,
    rk_ref,
    step_ref,
    pw_ref,
    slot_vmem,
    slot_ref,
    k_hi,
    k_lo,
    a_src,
    a_dst,
    b_src,
    b_dst,
    x_new,
    x_old,
    d_buf,
    u_buf,
    p_buf,
    n_buf,
    steps,
    weights,
    in_sem,
    out_sem,
    a_sem,
    b_sem,
    c_sem,
    f_sem,
    d_sem,
    p_sem,
    n_sem,
):
    me = lax.axis_index("rows")
    col = lax.axis_index("cols")
    core = lax.rem(me, 2)
    chip = lax.div(me, 2)
    sibling = me + 1 - 2 * core
    chips = R // 2
    row_blocks, slots, width = blocks_ref.shape[0], blocks_ref.shape[1], blocks_ref.shape[2]
    rows = row_blocks * width
    S = demand_ref.shape[0]
    H = HALVES
    n = S // H
    chunk = x_new.shape[3]
    tiles = chunk // width
    groups = S // SUB
    group = LANES // groups

    loads = []
    pairs = (
        (ids_hbm, ids_ref),
        (counts_hbm, counts_ref),
        (blocks_hbm.at[:, 0], blocks_ref),
        (step_hbm, step_ref),
        (pw_hbm, pw_ref),
        (obj_hbm, obj_ref),
        (lb_hbm, lb_ref),
        (ub_hbm, ub_ref),
        (vk_hbm, vk_ref),
        (demand_hbm, demand_ref),
        (rk_hbm, rk_ref),
    )
    for i, (src, dst) in enumerate(pairs):
        c = pltpu.make_async_copy(src, dst, in_sem.at[i])
        c.start()
        loads.append(c)

    barrier = pltpu.get_barrier_semaphore()
    for o in range(1, R):
        pl.semaphore_signal(barrier, inc=1, device_id={"rows": lax.rem(me + o, R)}, device_id_type=MESH)
    for o in range(1, C):
        pl.semaphore_signal(barrier, inc=1, device_id={"cols": lax.rem(col + o, C)}, device_id_type=MESH)

    loads[0].wait()
    loads[1].wait()
    lane4 = lax.broadcasted_iota(jnp.int32, (row_blocks, LANES), 1)
    slot_of = jnp.full((row_blocks, LANES), -1, jnp.int32)
    square = (row_blocks, row_blocks)
    same = lax.broadcasted_iota(jnp.int32, square, 0) == lax.broadcasted_iota(jnp.int32, square, 1)
    counts = jnp.broadcast_to(counts_ref[...], square).astype(f32)
    counts = jnp.sum(jnp.where(same, counts, 0.0), axis=1, keepdims=True)
    ids = ids_ref[:, 0, :]
    for w in range(slots):
        slot_of = jnp.where((ids[:, w : w + 1] == lane4) & (counts > w + 0.5), w, slot_of)
    slot_vmem[...] = slot_of
    c = pltpu.make_async_copy(slot_vmem, slot_ref, in_sem.at[len(pairs)])
    c.start()
    for load in loads[2:]:
        load.wait()
    c.wait()

    def copy(src, dst, sem, at, axis, target):
        return pltpu.make_async_remote_copy(
            src_ref=src,
            dst_ref=dst,
            send_sem=sem.at[(0,) + at],
            recv_sem=sem.at[(1,) + at],
            device_id={axis: target},
            device_id_type=MESH,
        )

    def chip_at(o):
        return lax.rem(chip + o, chips)

    def chip_from(o):
        return lax.rem(chip + chips - o, chips)

    eye = lax.broadcasted_iota(jnp.int32, (S, S), 0) == lax.broadcasted_iota(jnp.int32, (S, S), 1)

    def upright(ref):
        return jnp.sum(jnp.where(eye, jnp.broadcast_to(ref[...], (S, S)), 0.0), axis=1, keepdims=True)

    steps[...] = jnp.broadcast_to(upright(step_ref), (S, LANES))
    weights[...] = jnp.broadcast_to(upright(pw_ref), (S, LANES))
    lane = lax.broadcasted_iota(jnp.int32, (SUB, LANES), 1)

    def pack(parts):
        column = jnp.concatenate(parts, axis=0)
        tile = jnp.zeros((SUB, LANES), f32)
        for k in range(groups):
            tile = jnp.where(lax.div(lane, group) == k, column[k * SUB : (k + 1) * SUB], tile)
        return tile

    def project(values, at):
        lb, ub, kind = lb_ref[:, at], ub_ref[:, at], vk_ref[:, at]
        floored = jnp.maximum(values, lb)
        boxed = jnp.minimum(floored, ub)
        return jnp.where(kind == 0, values, jnp.where(kind == 1, floored, boxed))

    def columns(q):
        return pl.ds(pl.multiple_of(q * chunk, LANES), chunk)

    def half(h):
        return slice(h * n, (h + 1) * n)

    def forward(field, q):
        high, low = split(field)
        m = field.shape[0]
        both = matmul(jnp.concatenate([high, low], axis=0), k_hi[q], True)
        return both[:m] + both[m:] + matmul(high, k_lo[q], True)

    def give_total(h, parity, total):
        d_buf[parity, h, col] = total
        for o in range(1, C):
            block = d_buf.at[parity, h, col]
            copy(block, block, d_sem, (parity, h, o), "cols", lax.rem(col + o, C)).start()

    def give_primal(parity, parts):
        p_buf[parity, col] = pack(parts)
        for o in range(1, C):
            block = p_buf.at[parity, col]
            copy(block, block, p_sem, (parity, o), "cols", lax.rem(col + o, C)).start()

    def dual_half(h, parity):
        for o in range(1, C):
            block = d_buf.at[parity, h, lax.rem(col + C - o, C)]
            copy(block, block, d_sem, (parity, h, o), "cols", lax.rem(col + o, C)).wait_recv()
        image = d_buf[parity, h, 0]
        for k in range(1, C):
            image = image + d_buf[parity, h, k]
        sigma = (steps[half(h)] * weights[half(h)])[:, :1]
        old = u_buf[h]
        fresh = old + sigma * (demand_ref[half(h)] - image)
        fresh = jnp.where(rk_ref[...] == 1, jnp.maximum(fresh, 0.0), fresh)
        u_buf[h] = fresh
        return fresh, jnp.sum((fresh - old) ** 2, axis=1, keepdims=True)

    def give_norms(parity, dual_parts):
        for o in range(1, C):
            block = p_buf.at[parity, lax.rem(col + C - o, C)]
            copy(block, block, p_sem, (parity, o), "cols", lax.rem(col + o, C)).wait_recv()
        moved = p_buf[parity, 0]
        for k in range(1, C):
            moved = moved + p_buf[parity, k]
        n_buf[me] = jnp.where(lax.rem(lane, group) < group // 2, moved, pack(dual_parts))
        for o in range(1, R):
            copy(n_buf.at[me], n_buf.at[me], n_sem, (o,), "rows", lax.rem(me + o, R)).start()
        for o in range(1, C):
            block = p_buf.at[parity, col]
            copy(block, block, p_sem, (parity, o), "cols", lax.rem(col + o, C)).wait_send()
            for h in range(H):
                block = d_buf.at[parity, h, col]
                copy(block, block, d_sem, (parity, h, o), "cols", lax.rem(col + o, C)).wait_send()

    def take_norms():
        for o in range(1, R):
            block = n_buf.at[lax.rem(me + R - o, R)]
            copy(block, block, n_sem, (o,), "rows", lax.rem(me + o, R)).wait_recv()
        norms = n_buf[0]
        for r in range(1, R):
            norms = norms + n_buf[r]
        primal_move = jnp.concatenate([norms[:, k * group : k * group + 1] for k in range(groups)], axis=0)
        middle = group // 2
        dual_move = jnp.concatenate([norms[:, k * group + middle : k * group + middle + 1] for k in range(groups)], axis=0)
        ratio = (dual_move + EPS) / (primal_move + EPS)
        weights[...] = jnp.sqrt(weights[...] * jnp.broadcast_to(jnp.sqrt(ratio), (S, LANES)))
        for o in range(1, R):
            copy(n_buf.at[me], n_buf.at[me], n_sem, (o,), "rows", lax.rem(me + o, R)).wait_send()

    first_tau = (steps[...] / weights[...])[:, :1]

    def first(q, total):
        for r in range(row_blocks):
            for t in range(tiles):
                slot = slot_ref[r, q * tiles + t]
                tile = blocks_ref[r, jnp.maximum(slot, 0)]
                tile = jnp.where(slot >= 0, tile, 0.0)
                high, low = split(tile)
                k_hi[q, r * width : (r + 1) * width, t * width : (t + 1) * width] = high
                k_lo[q, r * width : (r + 1) * width, t * width : (t + 1) * width] = low
        at = columns(q)
        fresh = project(-first_tau * obj_ref[:, at], at)
        for h in range(H):
            x_old[h, q] = fresh[half(h)]
        return total + forward(2.0 * fresh, q)

    total = lax.fori_loop(0, R, first, jnp.zeros((S, rows), f32))
    pl.semaphore_wait(barrier, R + C - 2)
    for h in range(H):
        u_buf[h] = jnp.zeros((n, rows), f32)
        give_total(h, 0, total[half(h)])
    give_primal(0, [jnp.sum(x_old[h, me] ** 2, axis=1, keepdims=True) for h in range(H)])

    order = list(range(1, chips)) + [0]

    def iteration(step, carry):
        now = lax.rem(step, 2)
        sends = []

        def send(c):
            c.start()
            sends.append(c)

        def backward(both_dual, high, q):
            both = matmul(both_dual, k_hi[q], False)
            return both[:n] + both[n:] + matmul(high, k_lo[q], False)

        duals, dual_parts = [], []
        for h in range(H):
            dual, moved = dual_half(h, 1 - now)
            high, low = split(dual)
            both_dual = jnp.concatenate([high, low], axis=0)
            duals.append((both_dual, high))
            dual_parts.append(moved)
            for o in order:
                p = chip_at(o)
                a_src[h, o] = backward(both_dual, high, 2 * p + 1 - core)
                send(copy(a_src.at[h, o], a_dst.at[h, p], a_sem, (h, o), "rows", sibling))
        give_norms(1 - now, dual_parts)
        images = []
        for h in range(H):
            for o in order:
                p = chip_at(o)
                mine = backward(*duals[h], 2 * p + core)
                copy(a_src.at[h, o], a_dst.at[h, p], a_sem, (h, o), "rows", sibling).wait_recv()
                mine = mine + a_dst[h, p]
                if o > 0:
                    b_src[h, o] = mine
                    send(copy(b_src.at[h, o], b_dst.at[h, o], b_sem, (h, o), "rows", 2 * p + core))
            images.append(mine)
        take_norms()
        at = columns(me)
        primal_parts, fields = [], []
        for h in range(H):
            image = images[h]
            for o in range(1, chips):
                copy(b_src.at[h, o], b_dst.at[h, o], b_sem, (h, o), "rows", 2 * chip_at(o) + core).wait_recv()
                image = image + b_dst[h, o]
            tau = (steps[half(h)] / weights[half(h)])[:, :1]
            before = x_old[h, me]
            fresh = project(before - tau * (obj_ref[:, at] - image), at)
            block = x_new.at[h, me]
            block[...] = fresh
            for o in range(1, chips):
                send(copy(block, block, c_sem, (h, o), "rows", 2 * chip_at(o) + core))
            send(copy(block, block, c_sem, (h, 0), "rows", sibling))
            primal_parts.append(jnp.sum((fresh - before) ** 2, axis=1, keepdims=True))
            fields.append(2.0 * fresh - before)
            x_old[h, me] = fresh
        give_primal(now, primal_parts)
        totals = [forward(fields[h], me) for h in range(H)]

        def add(h, q):
            fresh = x_new[h, q]
            field = 2.0 * fresh - x_old[h, q]
            x_old[h, q] = fresh
            totals[h] = totals[h] + forward(field, q)

        for h in range(H):
            block = x_new.at[h, sibling]
            copy(block, block, c_sem, (h, 0), "rows", sibling).wait_recv()
            add(h, sibling)
        for h in range(H):
            for o in range(1, chips):
                q = 2 * chip_from(o) + core
                block = x_new.at[h, q]
                copy(block, block, c_sem, (h, o), "rows", 2 * chip_at(o) + core).wait_recv()
                send(copy(block, block, f_sem, (h, o), "rows", sibling))
                add(h, q)
        for h in range(H):
            for o in range(1, chips):
                q = 2 * chip_from(o) + 1 - core
                block = x_new.at[h, q]
                copy(block, block, f_sem, (h, o), "rows", sibling).wait_recv()
                add(h, q)
            give_total(h, now, totals[h])
        for c in sends:
            c.wait_send()
        return carry

    lax.fori_loop(1, ITERS, iteration, 0)
    stores = []
    for h in range(H):
        for q in range(R):
            c = pltpu.make_async_copy(x_old.at[h, q], x_hbm.at[half(h), q * chunk : (q + 1) * chunk], out_sem.at[h, q])
            c.start()
            stores.append(c)
    last = (ITERS - 1) % 2
    dual_parts = []
    for h in range(H):
        dual_parts.append(dual_half(h, last)[1])
    give_norms(last, dual_parts)
    for h in range(H):
        c = pltpu.make_async_copy(u_buf.at[h], u_hbm.at[half(h)], out_sem.at[h, R])
        c.start()
        stores.append(c)
    take_norms()
    final = jnp.broadcast_to(weights[:, :1], (S, S))
    w_ref[...] = jnp.sum(jnp.where(eye, final, 0.0), axis=0, keepdims=True)
    for c in stores:
        c.wait()


def hand_out(x_from, u_from, w_from, x_to, u_to, w_to, x_mid, u_mid, w_mid, sem):
    trips = ((x_from, x_mid, x_to), (u_from, u_mid, u_to), (w_from, w_mid, w_to))
    loads = [pltpu.make_async_copy(a, b, sem.at[0, i]) for i, (a, b, _) in enumerate(trips)]
    stores = [pltpu.make_async_copy(b, c, sem.at[1, i]) for i, (_, b, c) in enumerate(trips)]
    for c in loads:
        c.start()
    for load, store in zip(loads, stores):
        load.wait()
        store.start()
    for c in stores:
        c.wait()


def solution(mesh):
    R, C = mesh.shape["rows"], mesh.shape["cols"]

    def local(blocks, ell_index, counts, objective, lower, upper, var_kind, demand, row_kind, step_size, primal_weight):
        row_blocks, _, slots, width, _ = blocks.shape
        n_vars = objective.shape[0]
        S, rows = demand.shape
        H = HALVES
        n, chunk, chips = S // H, n_vars // R, R // 2
        hbm = pl.BlockSpec(memory_space=pltpu.HBM)
        primal, dual, weight = pl.pallas_call(
            functools.partial(kernel, R, C),
            out_shape=(
                jax.ShapeDtypeStruct((S, n_vars), f32),
                jax.ShapeDtypeStruct((S, rows), f32),
                jax.ShapeDtypeStruct((1, S), f32),
            ),
            in_specs=[hbm] * 11,
            out_specs=(hbm, hbm, pl.BlockSpec(memory_space=pltpu.VMEM)),
            scratch_shapes=[
                pltpu.VMEM((row_blocks, slots, width, width), f32),
                pltpu.VMEM(ell_index.shape, jnp.int32),
                pltpu.VMEM((1, row_blocks), jnp.int32),
                pltpu.VMEM((1, n_vars), f32),
                pltpu.VMEM((1, n_vars), f32),
                pltpu.VMEM((1, n_vars), f32),
                pltpu.VMEM((1, n_vars), jnp.int32),
                pltpu.VMEM((S, rows), f32),
                pltpu.VMEM((1, rows), jnp.int32),
                pltpu.VMEM((1, S), f32),
                pltpu.VMEM((1, S), f32),
                pltpu.VMEM((row_blocks, LANES), jnp.int32),
                pltpu.SMEM((row_blocks, LANES), jnp.int32),
                pltpu.VMEM((R, rows, chunk), bf16),
                pltpu.VMEM((R, rows, chunk), bf16),
                pltpu.VMEM((H, chips, n, chunk), f32),
                pltpu.VMEM((H, chips, n, chunk), f32),
                pltpu.VMEM((H, chips, n, chunk), f32),
                pltpu.VMEM((H, chips, n, chunk), f32),
                pltpu.VMEM((H, R, n, chunk), f32),
                pltpu.VMEM((H, R, n, chunk), f32),
                pltpu.VMEM((2, H, C, n, rows), f32),
                pltpu.VMEM((H, n, rows), f32),
                pltpu.VMEM((2, C, SUB, LANES), f32),
                pltpu.VMEM((R, SUB, LANES), f32),
                pltpu.VMEM((S, LANES), f32),
                pltpu.VMEM((S, LANES), f32),
                pltpu.SemaphoreType.DMA((12,)),
                pltpu.SemaphoreType.DMA((H, R + 1)),
                pltpu.SemaphoreType.DMA((2, H, chips)),
                pltpu.SemaphoreType.DMA((2, H, chips)),
                pltpu.SemaphoreType.DMA((2, H, chips)),
                pltpu.SemaphoreType.DMA((2, H, chips)),
                pltpu.SemaphoreType.DMA((2, 2, H, C)),
                pltpu.SemaphoreType.DMA((2, 2, C)),
                pltpu.SemaphoreType.DMA((2, R)),
            ],
            compiler_params=pltpu.CompilerParams(
                collective_id=0, has_side_effects=True, vmem_limit_bytes=64 * 1024 * 1024
            ),
        )(
            blocks,
            ell_index,
            counts.reshape(1, row_blocks),
            objective.reshape(1, n_vars),
            lower.reshape(1, n_vars),
            upper.reshape(1, n_vars),
            var_kind.reshape(1, n_vars),
            demand,
            row_kind.reshape(1, rows),
            step_size.reshape(1, S),
            primal_weight.reshape(1, S),
        )
        primal, dual, weight = pl.pallas_call(
            hand_out,
            out_shape=tuple(jax.ShapeDtypeStruct(a.shape, f32) for a in (primal, dual, weight)),
            in_specs=[hbm] * 3,
            out_specs=(hbm,) * 3,
            scratch_shapes=[
                pltpu.VMEM(primal.shape, f32),
                pltpu.VMEM(dual.shape, f32),
                pltpu.VMEM(weight.shape, f32),
                pltpu.SemaphoreType.DMA((2, 3)),
            ],
            compiler_params=pltpu.CompilerParams(vmem_limit_bytes=64 * 1024 * 1024),
        )(primal, dual, weight)
        return primal, dual, weight.reshape(S)

    return jax.shard_map(
        local,
        mesh=mesh,
        in_specs=(
            P("rows", "cols", None, None, None),
            P("rows", "cols", None),
            P("rows", "cols"),
            P("cols"),
            P("cols"),
            P("cols"),
            P("cols"),
            P(None, "rows"),
            P("rows"),
            P(),
            P(),
        ),
        out_specs=(P(None, "cols"), P(None, "rows"), P()),
        check_vma=False,
    )
```

time: 96.2 us -> 81.8 us (0.85)
  local copies, waits for them, and re-layouts: 9.82 us -> 0 us
  Pallas kernels: 83.6 us -> 81 us
  other arithmetic: 1.51 us -> 0 us
    unnamed x21 -> x0, local copies, waits for them, and re-layouts: 9.82 us -> none
    pallas_call x1, Pallas kernels: 83.6 us -> 79.1 us  [local(): pl.pallas_call(functools.partial(kernel, R, C), out_shape=(jax.ShapeDtype...]
    pallas_call x0 -> x1, Pallas kernels: none -> 1.9 us  [local(): pl.pallas_call(hand_out, out_shape=tuple((jax.ShapeDtypeStruct(a.shape, f...]
where the time goes in v2:
time: 81.8 us; the launch traced here: 81.6 us
  Pallas kernels  81 us (99%)
    pallas_call x1, Pallas kernels, local(): pl.pallas_call(functools.partial(kernel, R, C), out_shape=(jax.ShapeDtype...  79.1 us
    pallas_call x1, Pallas kernels, local(): pl.pallas_call(hand_out, out_shape=tuple((jax.ShapeDtypeStruct(a.shape, f...  1.9 us

profile of v2, /device:TPU:0, one launch (start us, length us, event | category | flops | bytes accessed | tf_op | source)
XLA Modules:
  0.0 81.6 jit_solution(509671389969723771)
XLA Ops:
  0.6 79.1 %shard_map.130 = (f32[32,4096]{1,0:T(8,128)}, f32[32,512]{1,0:T(8,128)}, f32[1,32]{1,0:T(1,128)}) custom-call(f32[4,1,16,128,128]{4,3,2,1,0:T(8,128)} %blocks_hbm.1, s32[4,1,16]{2,1,0:T(1,128)} %ids_hbm.1, s32[1,4]{1,0:T(1,128)} %bitcast.14, f32[1,4096]{1,0:T(1,128)} %bitcast.9, f32[1,4096]{1,0:T(1,128)} %bitcast.10, f32[1,4096]{1,0:T(1,128)} %bitcast.11, ...), custom_call_target="tpu_custom_call" | custom-call | tf_op jit(solution)/shard_map/pallas_call | solution.py:409
  79.7 1.9 %shard_map.131 = (f32[32,4096]{1,0:T(8,128)}, f32[32,512]{1,0:T(8,128)}, f32[1,32]{1,0:T(1,128)}) custom-call(f32[32,4096]{1,0:T(8,128)} %get-tuple-element.9.x_from, f32[32,512]{1,0:T(8,128)} %get-tuple-element.10.u_from, f32[1,32]{1,0:T(1,128)} %get-tuple-element.11.w_from), custom_call_target="tpu_custom_call" | custom-call | tf_op jit(solution)/shard_map/pallas_call | solution.py:472
